TPU v7x, 256 devices: a whole 4x4x8 slice. The times are simulated.
256 devices in a mesh: seq: 64 (over y_lo, x, z), dp: 4 (over y_hi, core).
Axes of the slice: x: 4, y: 4 (y_hi: 2, y_lo: 2; y = y_hi * 2 + y_lo), z: 8, core: 2. Of those that a mesh axis runs over, the one named last changes fastest.
Arguments:
- signal: float32 [4, 65536, 384], P('dp', 'seq'), may hold values from -6 to 6
- gate_values: float32 [4, 65536, 384], P('dp', 'seq'), may hold values from -6 to 6
- cotangent: float32 [4, 65536, 384], P('dp', 'seq'), may hold values from -6 to 6
- kernel: float32 [128, 512, 384], P(None, 'seq'), may hold values from -6 to 6
- first_factor: float32 [128, 128], replicated, may hold values from -0.5 to 0.5
- second_factor: float32 [512, 512], replicated, may hold values from -0.25 to 0.25
Outputs:
- grad_signal: float32 [4, 65536, 384], P('dp', 'seq')
- grad_gates: float32 [4, 65536, 384], P('dp', 'seq')
- grad_kernel: float32 [128, 512, 384], P('dp', 'seq')
- grad_first: float32 [128, 128], replicated
- grad_second: float32 [512, 512], replicated
All inputs are finite; a program needn't handle non-finite values.
Results may differ from a plain program's by a relative error of at most 0.000071.
Values sent between devices are 32-bit elements; how exact they have to be, the bound alone decides.
No kernel may reach another device: no remote copies, remote signals or barrier semaphores. Data moves between devices by JAX's collectives and lax.ppermute only.
A program may use at most 128 MiB of HBM per device.

v0:
```python
import math
import jax
import jax.numpy as jnp
from jax import lax
from jax.sharding import PartitionSpec as P


def along_second(data, factor):
    return jnp.einsum("bijc,kj->bikc", data, factor, precision=lax.Precision.HIGHEST)


def along_second_t(data, factor):
    return jnp.einsum("bikc,kj->bijc", data, factor, precision=lax.Precision.HIGHEST)


def along_first(factor, data):
    return jnp.einsum("mi,bikc->bmkc", factor, data, precision=lax.Precision.HIGHEST)


def along_first_t(factor, data):
    return jnp.einsum("mi,bmkc->bikc", factor, data, precision=lax.Precision.HIGHEST)


def outer_first(left, right):
    return jnp.einsum("bmkc,bikc->mi", left, right, precision=lax.Precision.HIGHEST)


def outer_second(left, right):
    return jnp.einsum("bikc,bijc->kj", left, right, precision=lax.Precision.HIGHEST)


def body(signal, gate_values, cotangent, kernel, first_factor, second_factor):
    batch = signal.shape[0]
    blocks = first_factor.shape[0]
    block = second_factor.shape[0]
    channels = signal.shape[2]
    local_rows = signal.shape[1] // block
    shape_rows = (batch, local_rows, block, channels)
    source = signal.reshape(shape_rows)
    gating = gate_values.reshape(shape_rows)
    upstream = cotangent.reshape(shape_rows)
    whole = lax.all_to_all(source, "seq", split_axis=3, concat_axis=1, tiled=True)
    kernel_cols = lax.all_to_all(kernel, "seq", split_axis=2, concat_axis=1, tiled=True)
    section_one = along_second(whole, second_factor)
    spectrum = along_first(first_factor, section_one)
    weighted = kernel_cols[None] * spectrum
    back_one = along_first_t(first_factor, weighted)
    full_mixed = along_second_t(back_one, second_factor)
    mixed = lax.all_to_all(full_mixed, "seq", split_axis=1, concat_axis=3, tiled=True)
    grad_mixed = upstream * gating
    grad_gate = upstream * mixed
    grad_whole = lax.all_to_all(grad_mixed, "seq", split_axis=3, concat_axis=1, tiled=True)
    grad_back = along_second(grad_whole, second_factor)
    second_grad = outer_second(back_one, grad_whole)
    grad_weighted = along_first(first_factor, grad_back)
    first_grad = outer_first(weighted, grad_back)
    kernel_cols_grad = jnp.sum(grad_weighted * spectrum, axis=0)
    grad_spectrum = grad_weighted * kernel_cols[None]
    grad_section = along_first_t(first_factor, grad_spectrum)
    first_grad = first_grad + outer_first(grad_spectrum, section_one)
    grad_full = along_second_t(grad_section, second_factor)
    second_grad = second_grad + outer_second(grad_section, whole)
    grad_source = lax.all_to_all(grad_full, "seq", split_axis=1, concat_axis=3, tiled=True)
    kernel_term = lax.all_to_all(kernel_cols_grad, "seq", split_axis=1, concat_axis=2, tiled=True)
    grad_kernel = lax.psum_scatter(kernel_term, "dp", scatter_dimension=0, tiled=True)
    first_total, second_total = lax.psum((first_grad, second_grad), ("seq", "dp"))
    sequences = batch * lax.axis_size("dp")
    first_scale = 1.0 / math.sqrt(sequences * block * channels)
    second_scale = 1.0 / math.sqrt(sequences * blocks * channels)
    return (
        grad_source.reshape(signal.shape),
        grad_gate.reshape(signal.shape),
        grad_kernel,
        first_total * first_scale,
        second_total * second_scale,
    )


def solution(mesh):
    in_specs = (
        P("dp", "seq", None),
        P("dp", "seq", None),
        P("dp", "seq", None),
        P(None, "seq", None),
        P(),
        P(),
    )
    out_specs = (P("dp", "seq", None), P("dp", "seq", None), P("dp", "seq", None), P(), P())
    return jax.shard_map(body, mesh=mesh, in_specs=in_specs, out_specs=out_specs, check_vma=False)
```

profile of v0, /device:TPU:6, one launch (start us, length us, event | category | flops | bytes accessed | tf_op | source)
XLA Modules:
  0.0 535.5 jit_solution(2666855981043520354)
XLA Ops:
  8.0 3.8 copy.114
  11.8 13.0 %all-to-all-start.3 = ((f32[1,2,512,384]{2,1,0,3:T(2,128)}), f32[1,2,512,384]{2,1,0,3:T(2,128)S(1)}, u32[]{:S(2)}, u32[]{:S(2)}) async-start(f32[1,2,512,384]{2,1,0,3:T(2,128)} %copy.114), calls=%async_computation.3 | async-start | bytes 3145728 | tf_op jit(solution)/shard_map/all_to_all | solution.py:42
  24.8 3.2 mul.41
  28.0 3.7 copy.113
  31.7 32.9 %all-to-all-done.3 = f32[1,2,512,384]{2,1,0,3:T(2,128)S(1)} async-done(((f32[1,2,512,384]{2,1,0,3:T(2,128)}), f32[1,2,512,384]{2,1,0,3:T(2,128)S(1)}, u32[]{:S(2)}, u32[]{:S(2)}) %all-to-all-start.3) | async-done | bytes 1572896 | tf_op jit(solution)/shard_map/all_to_all | solution.py:42
  64.6 6.6 %all-to-all-start = ((f32[1,2,512,384]{2,1,0,3:T(2,128)}), f32[1,2,512,384]{2,1,0,3:T(2,128)}, u32[]{:S(2)}, u32[]{:S(2)}) async-start(f32[1,2,512,384]{2,1,0,3:T(2,128)} %copy.113), calls=%async_computation | async-start | bytes 3145728 | tf_op jit(solution)/shard_map/all_to_all | solution.py:52
  71.2 3.1 copy.87
  74.3 35.7 %all-to-all-done = f32[1,2,512,384]{2,1,0,3:T(2,128)} async-done(((f32[1,2,512,384]{2,1,0,3:T(2,128)}), f32[1,2,512,384]{2,1,0,3:T(2,128)}, u32[]{:S(2)}, u32[]{:S(2)}) %all-to-all-start) | async-done | bytes 1572896 | tf_op jit(solution)/shard_map/all_to_all | solution.py:52
  110.0 6.3 %all-to-all-start.1 = ((f32[128,8,384]{0,1,2:T(8,128)}), f32[128,8,384]{0,1,2:T(8,128)S(1)}, u32[]{:S(2)}, u32[]{:S(2)}) async-start(f32[128,8,384]{0,1,2:T(8,128)} %copy.87), calls=%async_computation.1 | async-start | bytes 3145728 | tf_op jit(solution)/shard_map/all_to_all | solution.py:43
  116.3 3.1 copy.93
  119.4 3.1 reshape.99
  122.5 3.1 copy.85
  125.6 3.3 reshape.93
  129.0 4.2 fusion.44
  133.2 1.5 fusion.10
  135.2 2.7 fusion.47
  137.9 2.6 fusion.14
  141.6 2.2 copy.98
  143.9 10.8 %all-to-all-done.1 = f32[128,8,384]{0,1,2:T(8,128)S(1)} async-done(((f32[128,8,384]{0,1,2:T(8,128)}), f32[128,8,384]{0,1,2:T(8,128)S(1)}, u32[]{:S(2)}, u32[]{:S(2)}) %all-to-all-start.1) | async-done | bytes 1572896 | tf_op jit(solution)/shard_map/all_to_all | solution.py:43
  154.6 6.9 %all-to-all-start.5 = ((f32[128,512,6]{0,2,1:T(8,128)}), f32[128,512,6]{0,2,1:T(8,128)}, u32[]{:S(2)}, u32[]{:S(2)}) async-start(f32[128,512,6]{0,2,1:T(8,128)} %copy.98), calls=%async_computation.5 | async-start | bytes 4194304 | tf_op jit(solution)/shard_map/all_to_all | solution.py:64
  161.5 2.8 fusion.53
  165.5 2.7 fusion.19
  168.2 2.9 copy.95
  171.1 38.3 %all-to-all-done.5 = f32[128,512,6]{0,2,1:T(8,128)} async-done(((f32[128,512,6]{0,2,1:T(8,128)}), f32[128,512,6]{0,2,1:T(8,128)}, u32[]{:S(2)}, u32[]{:S(2)}) %all-to-all-start.5) | async-done | bytes 1572896 | tf_op jit(solution)/shard_map/all_to_all | solution.py:64
  209.4 6.8 %all-to-all-start.4 = ((f32[1,128,512,6]{2,0,3,1:T(1,128)}), f32[1,128,512,6]{2,0,3,1:T(1,128)}, u32[]{:S(2)}, u32[]{:S(2)}) async-start(f32[1,128,512,6]{2,0,3,1:T(1,128)} %copy.95), calls=%async_computation.4 | async-start | bytes 3145728 | tf_op jit(solution)/shard_map/all_to_all | solution.py:49
  216.6 4.7 fusion.25
  221.4 2.7 fusion.34
  224.1 1.4 fusion.50
  225.6 3.4 fusion.40
  229.0 3.7 fusion.31
  232.9 1.9 copy.100
  234.9 1.8 copy.101
  236.7 1.4 copy-done.12
  238.1 2.7 fusion.22
  240.7 2.8 copy.90
  243.5 9.3 %all-to-all-done.4 = f32[1,128,512,6]{2,0,3,1:T(1,128)} async-done(((f32[1,128,512,6]{2,0,3,1:T(1,128)}), f32[1,128,512,6]{2,0,3,1:T(1,128)}, u32[]{:S(2)}, u32[]{:S(2)}) %all-to-all-start.4) | async-done | bytes 1572896 | tf_op jit(solution)/shard_map/all_to_all | solution.py:49
  252.7 6.8 %all-to-all-start.2 = ((f32[1,128,512,6]{2,0,3,1:T(1,128)}), f32[1,128,512,6]{2,0,3,1:T(1,128)S(1)}, u32[]{:S(2)}, u32[]{:S(2)}) async-start(f32[1,128,512,6]{2,0,3,1:T(1,128)} %copy.90), calls=%async_computation.2 | async-start | bytes 3145728 | tf_op jit(solution)/shard_map/all_to_all | solution.py:63
  259.6 3.0 copy.97
  262.6 242.0 %all-reduce.3.cloned.1.call-done = (f32[128,128]{1,0:T(8,128)}, f32[512,512]{1,0:T(8,128)}) async-done(((f32[128,128]{1,0:T(8,128)}, f32[512,512]{1,0:T(8,128)}), (f32[128,128]{1,0:T(8,128)}, f32[512,512]{1,0:T(8,128)})) %all-reduce.3.cloned.1.call-update) | async-done | bytes 1114128 | tf_op jit(solution)/shard_map/psum | solution.py:66
  504.6 1.5 broadcast_multiply_fusion.1
  506.1 2.3 broadcast_multiply_fusion
  508.4 3.4 copy.124
  511.8 3.4 all_to_all.85
  515.2 3.4 mul.45
  518.6 3.0 copy.106
  521.6 2.0 copy.125
  523.5 2.6 reshape.97
  526.2 1.6 copy.105
  (38 shorter events, 3.6 us)
Async XLA Ops:
  8.0 120.9 %copy-start = (f32[512,512]{1,0:T(8,128)S(1)}, f32[512,512]{1,0:T(8,128)}, u32[]{:S(2)}) copy-start(f32[512,512]{1,0:T(8,128)} %param.11) | copy-start | bytes 3145732
  11.8 52.8 %all-to-all-start.3 = ((f32[1,2,512,384]{2,1,0,3:T(2,128)}), f32[1,2,512,384]{2,1,0,3:T(2,128)S(1)}, u32[]{:S(2)}, u32[]{:S(2)}) async-start(f32[1,2,512,384]{2,1,0,3:T(2,128)} %copy.114), calls=%async_computation.3 | async-start | bytes 3145728 | tf_op jit(solution)/shard_map/all_to_all | solution.py:42
  64.6 9.7 %copy-start.14 = (f32[1,2,512,384]{2,1,0,3:T(2,128)}, f32[1,2,512,384]{2,1,0,3:T(2,128)S(1)}, u32[]{:S(2)}) copy-start(f32[1,2,512,384]{2,1,0,3:T(2,128)S(1)} %all-to-all-done.3) | copy-start | bytes 4718596
  64.6 45.4 %all-to-all-start = ((f32[1,2,512,384]{2,1,0,3:T(2,128)}), f32[1,2,512,384]{2,1,0,3:T(2,128)}, u32[]{:S(2)}, u32[]{:S(2)}) async-start(f32[1,2,512,384]{2,1,0,3:T(2,128)} %copy.113), calls=%async_computation | async-start | bytes 3145728 | tf_op jit(solution)/shard_map/all_to_all | solution.py:52
  110.0 44.6 %all-to-all-start.1 = ((f32[128,8,384]{0,1,2:T(8,128)}), f32[128,8,384]{0,1,2:T(8,128)S(1)}, u32[]{:S(2)}, u32[]{:S(2)}) async-start(f32[128,8,384]{0,1,2:T(8,128)} %copy.87), calls=%async_computation.1 | async-start | bytes 3145728 | tf_op jit(solution)/shard_map/all_to_all | solution.py:43
  128.9 4.2 copy-start.15
  133.2 1.5 copy-start.6
  133.2 2.0 copy-start.8
  135.2 5.3 copy-start.3
  137.8 2.6 copy-start.9
  140.5 1.1 copy-start.1
  154.6 54.7 %all-to-all-start.5 = ((f32[128,512,6]{0,2,1:T(8,128)}), f32[128,512,6]{0,2,1:T(8,128)}, u32[]{:S(2)}, u32[]{:S(2)}) async-start(f32[128,512,6]{0,2,1:T(8,128)} %copy.98), calls=%async_computation.5 | async-start | bytes 4194304 | tf_op jit(solution)/shard_map/all_to_all | solution.py:64
  164.3 1.2 copy-start.13
  209.4 43.4 %all-to-all-start.4 = ((f32[1,128,512,6]{2,0,3,1:T(1,128)}), f32[1,128,512,6]{2,0,3,1:T(1,128)}, u32[]{:S(2)}, u32[]{:S(2)}) async-start(f32[1,128,512,6]{2,0,3,1:T(1,128)} %copy.95), calls=%async_computation.4 | async-start | bytes 3145728 | tf_op jit(solution)/shard_map/all_to_all | solution.py:49
  216.2 288.4 %all-reduce.3.cloned.1.call-start = ((), (), s32[]{:S(2)}) async-start(), calls=%async_computation.8 | async-start | bytes 2228224 | tf_op jit(solution)/shard_map/psum | solution.py:66
  216.6 4.7 copy-start.4
  216.6 4.7 copy-start.10
  221.4 2.7 copy-start.2
  224.1 1.4 copy-start.7
  225.6 3.4 copy-start.11
  225.6 3.4 copy-start.5
  232.7 295.1 %reduce-scatter.2.cloned.1.call-start = ((), (), s32[]{:S(2)}) async-start(), calls=%async_computation.7 | async-start | bytes 1966080 | tf_op jit(solution)/shard_map/reduce_scatter | solution.py:65
  236.7 1.4 copy-start.12
  252.7 268.8 %all-to-all-start.2 = ((f32[1,128,512,6]{2,0,3,1:T(1,128)}), f32[1,128,512,6]{2,0,3,1:T(1,128)S(1)}, u32[]{:S(2)}, u32[]{:S(2)}) async-start(f32[1,128,512,6]{2,0,3,1:T(1,128)} %copy.90), calls=%async_computation.2 | async-start | bytes 3145728 | tf_op jit(solution)/shard_map/all_to_all | solution.py:63
Sparse Core Ops, SparseCore 0:
  232.8 271.7 all-reduce.2
Sparse Core Ops, SparseCore 1:
  236.8 48.6 reduce-scatter.1
where the time goes:
time: 543 us; the launch traced here: 535 us
  waiting for transfers between devices  369 us (68%)
  local copies, waits for them, and re-layouts  57.9 us (11%)
  starting transfers between devices  47 us (9%)
  matrix products  35 us (6%)
  between operations  16 us (3%)
  other arithmetic  10.5 us (2%)
    psum x1, waiting for transfers between devices, body(): lax.psum((first_grad, second_grad), ('seq', 'dp'))  242 us
    all_to_all x1, waiting for transfers between devices, body(): lax.all_to_all(kernel_cols_grad, 'seq', split_axis=1, concat_axis=2, tile...  38.3 us
    all_to_all x1, waiting for transfers between devices, body(): lax.all_to_all(grad_mixed, 'seq', split_axis=3, concat_axis=1, tiled=True)  35.7 us
    all_to_all x1, waiting for transfers between devices, body(): lax.all_to_all(source, 'seq', split_axis=3, concat_axis=1, tiled=True)  32.9 us
    unnamed x36, local copies, waits for them, and re-layouts  14.9 us
    all_to_all x1, starting transfers between devices, body(): lax.all_to_all(source, 'seq', split_axis=3, concat_axis=1, tiled=True)  13 us
  transfers between devices with their start and end apart: 8, of which 6 were waited for; matrix products, arithmetic and copies ran while one was open for 17% of the time, Pallas kernels for 0%

commit v1 on v0

--- a/solution.py
+++ b/solution.py
@@ -63,7 +63,7 @@
     grad_source = lax.all_to_all(grad_full, "seq", split_axis=1, concat_axis=3, tiled=True)
     kernel_term = lax.all_to_all(kernel_cols_grad, "seq", split_axis=1, concat_axis=2, tiled=True)
     grad_kernel = lax.psum_scatter(kernel_term, "dp", scatter_dimension=0, tiled=True)
-    first_total, second_total = lax.psum((first_grad, second_grad), ("seq", "dp"))
+    first_total, second_total = lax.psum(lax.psum((first_grad, second_grad), "dp"), "seq")
     sequences = batch * lax.axis_size("dp")
     first_scale = 1.0 / math.sqrt(sequences * block * channels)
     second_scale = 1.0 / math.sqrt(sequences * blocks * channels)

time: 543 us -> 920 us (1.69)
  waiting for transfers between devices: 369 us -> 744 us
    psum x1 -> x2, waiting for transfers between devices: 242 us -> 605 us  [the longest x1 551 us: body(): lax.psum(lax.psum((first_grad, second_grad), 'dp'), 'seq')]
    reduce_scatter x1, waiting for transfers between devices: 0.01 us -> 27 us  [body(): lax.psum_scatter(kernel_term, 'dp', scatter_dimension=0, tiled=True)]
    all_to_all x1, waiting for transfers between devices: 9.26 us -> 0.01 us  [body(): lax.all_to_all(full_mixed, 'seq', split_axis=1, concat_axis=3, tiled=True)]
  transfers between devices with their start and end apart: 8 -> 9, of which waited for: 6 -> 7; matrix products, arithmetic and copies ran while one was open for 17% -> 10% of each run, Pallas kernels for 0% -> 0%
where the time goes in v1:
time: 920 us; the launch traced here: 912 us
  waiting for transfers between devices  744 us (81%)
  local copies, waits for them, and re-layouts  57.8 us (6%)
  starting transfers between devices  50.7 us (6%)
  matrix products  34.5 us (4%)
  between operations  14.3 us (2%)
  other arithmetic  10.5 us (1%)
    psum x1, waiting for transfers between devices, body(): lax.psum(lax.psum((first_grad, second_grad), 'dp'), 'seq')  551 us
    psum x1, waiting for transfers between devices, body(): lax.psum((first_grad, second_grad), 'dp')  54.5 us
    all_to_all x1, waiting for transfers between devices, body(): lax.all_to_all(grad_mixed, 'seq', split_axis=3, concat_axis=1, tiled=True)  35.8 us
    all_to_all x1, waiting for transfers between devices, body(): lax.all_to_all(source, 'seq', split_axis=3, concat_axis=1, tiled=True)  32.9 us
    all_to_all x1, waiting for transfers between devices, body(): lax.all_to_all(kernel_cols_grad, 'seq', split_axis=1, concat_axis=2, tile...  32.3 us
    reduce_scatter x1, waiting for transfers between devices, body(): lax.psum_scatter(kernel_term, 'dp', scatter_dimension=0, tiled=True)  27 us
  transfers between devices with their start and end apart: 9, of which 7 were waited for; matrix products, arithmetic and copies ran while one was open for 10% of the time, Pallas kernels for 0%

profile of v1, /device:TPU:6, one launch (start us, length us, event | category | flops | bytes accessed | tf_op | source)
XLA Modules:
  0.0 911.9 jit_solution(17431046730313779515)
XLA Ops:
  7.2 3.8 copy.114
  10.9 13.0 %all-to-all-start.3 = ((f32[1,2,512,384]{2,1,0,3:T(2,128)}), f32[1,2,512,384]{2,1,0,3:T(2,128)S(1)}, u32[]{:S(2)}, u32[]{:S(2)}) async-start(f32[1,2,512,384]{2,1,0,3:T(2,128)} %copy.114), calls=%async_computation.3 | async-start | bytes 3145728 | tf_op jit(solution)/shard_map/all_to_all | solution.py:42
  24.0 3.2 mul.41
  27.1 3.7 copy.113
  30.8 32.9 %all-to-all-done.3 = f32[1,2,512,384]{2,1,0,3:T(2,128)S(1)} async-done(((f32[1,2,512,384]{2,1,0,3:T(2,128)}), f32[1,2,512,384]{2,1,0,3:T(2,128)S(1)}, u32[]{:S(2)}, u32[]{:S(2)}) %all-to-all-start.3) | async-done | bytes 1572896 | tf_op jit(solution)/shard_map/all_to_all | solution.py:42
  63.7 6.6 all-to-all-start
  70.3 3.0 copy.87
  73.4 35.8 %all-to-all-done = f32[1,2,512,384]{2,1,0,3:T(2,128)} async-done(((f32[1,2,512,384]{2,1,0,3:T(2,128)}), f32[1,2,512,384]{2,1,0,3:T(2,128)}, u32[]{:S(2)}, u32[]{:S(2)}) %all-to-all-start) | async-done | bytes 1572896 | tf_op jit(solution)/shard_map/all_to_all | solution.py:52
  109.2 6.3 all-to-all-start.1
  115.5 3.1 copy.93
  118.5 3.1 reshape.99
  121.7 3.1 copy.85
  124.8 3.3 reshape.93
  128.1 4.2 fusion.44
  132.3 1.5 fusion.10
  134.3 2.7 fusion.47
  137.0 2.6 fusion.14
  140.8 2.3 copy.98
  143.1 10.7 %all-to-all-done.1 = f32[128,8,384]{0,1,2:T(8,128)S(1)} async-done(((f32[128,8,384]{0,1,2:T(8,128)}), f32[128,8,384]{0,1,2:T(8,128)S(1)}, u32[]{:S(2)}, u32[]{:S(2)}) %all-to-all-start.1) | async-done | bytes 1572896 | tf_op jit(solution)/shard_map/all_to_all | solution.py:43
  153.8 6.9 all-to-all-start.5
  160.7 2.8 fusion.53
  164.7 2.7 fusion.19
  167.4 2.8 copy.95
  170.2 2.6 fusion.34
  172.9 3.4 fusion.40
  176.2 32.3 %all-to-all-done.5 = f32[128,512,6]{0,2,1:T(8,128)} async-done(((f32[128,512,6]{0,2,1:T(8,128)}), f32[128,512,6]{0,2,1:T(8,128)}, u32[]{:S(2)}, u32[]{:S(2)}) %all-to-all-start.5) | async-done | bytes 1572896 | tf_op jit(solution)/shard_map/all_to_all | solution.py:64
  208.5 6.8 all-to-all-start.4
  215.4 3.0 fusion.50
  218.4 2.7 fusion.25
  221.1 3.7 fusion.31
  224.9 54.5 %all-reduce.7.cloned.1.call-done = (f32[128,128]{1,0:T(8,128)}, f32[512,512]{1,0:T(8,128)}) async-done(((f32[128,128]{1,0:T(8,128)}, f32[512,512]{1,0:T(8,128)}), (f32[128,128]{1,0:T(8,128)}, f32[512,512]{1,0:T(8,128)})) %all-reduce.7.cloned.1.call-update) | async-done | bytes 1114128 | tf_op jit(solution)/shard_map/psum | solution.py:66
  279.7 1.9 copy.100
  281.6 1.8 copy.101
  284.8 2.6 fusion.22
  287.4 2.8 copy.90
  290.2 10.9 %all-to-all-start.2 = ((f32[1,128,512,6]{2,0,3,1:T(1,128)}), f32[1,128,512,6]{2,0,3,1:T(1,128)S(1)}, u32[]{:S(2)}, u32[]{:S(2)}) async-start(f32[1,128,512,6]{2,0,3,1:T(1,128)} %copy.90), calls=%async_computation.2 | async-start | bytes 3145728 | tf_op jit(solution)/shard_map/all_to_all | solution.py:63
  301.1 3.0 copy.97
  304.1 550.9 %all-reduce.5.cloned.1.call-done = (f32[128,128]{1,0:T(8,128)}, f32[512,512]{1,0:T(8,128)}) async-done(((f32[128,128]{1,0:T(8,128)}, f32[512,512]{1,0:T(8,128)}), (f32[128,128]{1,0:T(8,128)}, f32[512,512]{1,0:T(8,128)})) %all-reduce.5.cloned.1.call-update) | async-done | bytes 1114128 | tf_op jit(solution)/shard_map/psum | solution.py:66
  855.0 1.5 broadcast_multiply_fusion.1
  856.5 2.3 broadcast_multiply_fusion
  858.8 3.4 copy.124
  862.2 3.4 all_to_all.85
  865.6 3.4 mul.45
  869.0 3.0 copy.106
  872.0 2.0 copy.125
  874.0 2.6 reshape.97
  876.6 1.6 copy.105
  878.2 27.0 %reduce-scatter.2.cloned.1.call-done = f32[32,8,384]{2,1,0:T(8,128)} async-done(((f32[128,8,384]{2,1,0:T(8,128)}), f32[32,8,384]{2,1,0:T(8,128)}) %reduce-scatter.2.cloned.1.call-update) | async-done | bytes 393232 | tf_op jit(solution)/shard_map/reduce_scatter | solution.py:65
  (45 shorter events, 4.6 us)
Async XLA Ops:
  7.2 120.9 %copy-start = (f32[512,512]{1,0:T(8,128)S(1)}, f32[512,512]{1,0:T(8,128)}, u32[]{:S(2)}) copy-start(f32[512,512]{1,0:T(8,128)} %param.11) | copy-start | bytes 3145732
  10.9 52.8 %all-to-all-start.3 = ((f32[1,2,512,384]{2,1,0,3:T(2,128)}), f32[1,2,512,384]{2,1,0,3:T(2,128)S(1)}, u32[]{:S(2)}, u32[]{:S(2)}) async-start(f32[1,2,512,384]{2,1,0,3:T(2,128)} %copy.114), calls=%async_computation.3 | async-start | bytes 3145728 | tf_op jit(solution)/shard_map/all_to_all | solution.py:42
  63.7 9.6 %copy-start.16 = (f32[1,2,512,384]{2,1,0,3:T(2,128)}, f32[1,2,512,384]{2,1,0,3:T(2,128)S(1)}, u32[]{:S(2)}) copy-start(f32[1,2,512,384]{2,1,0,3:T(2,128)S(1)} %all-to-all-done.3) | copy-start | bytes 4718596
  63.7 45.4 %all-to-all-start = ((f32[1,2,512,384]{2,1,0,3:T(2,128)}), f32[1,2,512,384]{2,1,0,3:T(2,128)}, u32[]{:S(2)}, u32[]{:S(2)}) async-start(f32[1,2,512,384]{2,1,0,3:T(2,128)} %copy.113), calls=%async_computation | async-start | bytes 3145728 | tf_op jit(solution)/shard_map/all_to_all | solution.py:52
  109.2 44.6 %all-to-all-start.1 = ((f32[128,8,384]{0,1,2:T(8,128)}), f32[128,8,384]{0,1,2:T(8,128)S(1)}, u32[]{:S(2)}, u32[]{:S(2)}) async-start(f32[128,8,384]{0,1,2:T(8,128)} %copy.87), calls=%async_computation.1 | async-start | bytes 3145728 | tf_op jit(solution)/shard_map/all_to_all | solution.py:43
  128.1 4.2 copy-start.17
  132.3 1.5 copy-start.8
  132.3 2.0 copy-start.6
  134.3 5.3 copy-start.3
  137.0 2.6 copy-start.10
  139.6 1.1 copy-start.1
  153.8 54.7 %all-to-all-start.5 = ((f32[128,512,6]{0,2,1:T(8,128)}), f32[128,512,6]{0,2,1:T(8,128)}, u32[]{:S(2)}, u32[]{:S(2)}) async-start(f32[128,512,6]{0,2,1:T(8,128)} %copy.98), calls=%async_computation.5 | async-start | bytes 4194304 | tf_op jit(solution)/shard_map/all_to_all | solution.py:64
  163.5 1.2 copy-start.14
  167.4 2.8 copy-start.4
  167.4 2.8 copy-start.11
  170.2 2.7 copy-start.2
  170.2 2.7 copy-start.9
  208.5 81.7 %all-to-all-start.4 = ((f32[1,128,512,6]{2,0,3,1:T(1,128)}), f32[1,128,512,6]{2,0,3,1:T(1,128)}, u32[]{:S(2)}, u32[]{:S(2)}) async-start(f32[1,128,512,6]{2,0,3,1:T(1,128)} %copy.95), calls=%async_computation.4 | async-start | bytes 3145728 | tf_op jit(solution)/shard_map/all_to_all | solution.py:49
  215.3 64.1 %all-reduce.7.cloned.1.call-start = ((), (), s32[]{:S(2)}) async-start(), calls=%async_computation.9 | async-start | bytes 2228224 | tf_op jit(solution)/shard_map/psum | solution.py:66
  215.4 3.0 copy-start.7
  215.4 3.0 copy-start.15
  218.4 2.7 copy-start.12
  218.4 2.7 copy-start.5
  224.8 630.2 %all-reduce.5.cloned.1.call-start = ((), (), s32[]{:S(2)}) async-start(), calls=%async_computation.8 | async-start | bytes 2228224 | tf_op jit(solution)/shard_map/psum | solution.py:66
  279.4 625.8 %reduce-scatter.2.cloned.1.call-start = ((), (), s32[]{:S(2)}) async-start(), calls=%async_computation.7 | async-start | bytes 1966080 | tf_op jit(solution)/shard_map/reduce_scatter | solution.py:65
  283.4 1.4 copy-start.13
  290.2 581.8 %all-to-all-start.2 = ((f32[1,128,512,6]{2,0,3,1:T(1,128)}), f32[1,128,512,6]{2,0,3,1:T(1,128)S(1)}, u32[]{:S(2)}, u32[]{:S(2)}) async-start(f32[1,128,512,6]{2,0,3,1:T(1,128)} %copy.90), calls=%async_computation.2 | async-start | bytes 3145728 | tf_op jit(solution)/shard_map/all_to_all | solution.py:63
Sparse Core Ops, SparseCore 0:
  225.0 54.3 all-reduce.6
  282.3 572.6 all-reduce.4
  858.4 46.7 reduce-scatter.1
